TPU v7x, 32 devices: a whole 2x2x4 slice. The times are simulated.
32 devices in a mesh: groups: 2 (over x), aux: 8 (over z, y), bas: 2 (over core).
Axes of the slice: x: 2, y: 2, z: 4, core: 2. Of those that a mesh axis runs over, the one named last changes fastest.
Arguments:
- factors: bfloat16 [128, 16, 4, 128, 128], P(('groups', 'aux'), 'bas'), parts along dimension 0, may hold values from -6 to 6
- tile_cols: int32 [32, 4], P(('groups', 'bas')), parts along dimension 0, may hold values from 0 to 15, as said below
- tile_live: int32 [32, 4], P(('groups', 'bas')), parts along dimension 0, may hold values from 0 to 1, as said below
- coefficients: bfloat16 [1024, 2048], P('groups'), parts along dimension 0, may hold values from -0.25 to 0.25
- batch_rows: int32 [4, 128], P('groups'), parts along dimension 0, may hold values from 0 to 511, as said below
Outputs:
- exchange: float32 [4096, 2048], P(('groups', 'bas'), 'aux'), parts along dimension 0
There are 2 independent parts, one for each index of `groups`. A program takes and returns all parts, laid end to end along the dimension named above; each array names one. Nothing has to cross between parts.
Inputs may be any that keep to these rules, and one draw needn't show every extreme that they name: `tile_cols`: in each row t the 4 column tiles are distinct and slot 0 holds t itself. `tile_live`: slot 0 of every row is live. `batch_rows`: all 256 entries are distinct.
All inputs are finite; a program needn't handle non-finite values.
Results may differ from a plain program's by a relative error of at most 0.0014.
Values may be sent and summed in bfloat16 or wider, within the bound.
A program may use at most 128 MiB of HBM per device.

v0:
```python
import math

import jax
import jax.numpy as jnp
from jax import lax
from jax.sharding import PartitionSpec as P


def on_device(factors, tile_cols, tile_live, coefficients, batch_rows):
    tile_width = factors.shape[3]
    own_tiles = factors.shape[1]
    aux_local = factors.shape[0]
    orbital_count = batch_rows.shape[1]
    batch_count = batch_rows.shape[0]
    tiles_all = coefficients.shape[1] // tile_width
    live_mask = tile_live.astype(jnp.bfloat16)
    norm_factor = 1.0 / math.sqrt(aux_local * lax.axis_size("aux") * batch_count * orbital_count)
    result = None
    for batch in range(batch_count):
        orbital_rows = coefficients[batch_rows[batch]].reshape(orbital_count, tiles_all, tile_width)
        picked = orbital_rows[:, tile_cols, :] * live_mask[None, :, :, None]
        half_done = jnp.einsum(
            "ptkxy,itky->iptx", factors, picked, preferred_element_type=jnp.float32
        )
        source = half_done.astype(jnp.bfloat16).reshape(
            orbital_count, aux_local, own_tiles * tile_width
        )
        partial_value = lax.dot_general(
            source,
            lax.all_gather(source, "bas", axis=2, tiled=True),
            (((0, 1), (0, 1)), ((), ())),
            preferred_element_type=jnp.float32,
        )
        reduced = lax.psum_scatter(partial_value, "aux", scatter_dimension=1, tiled=True)
        result = reduced if result is None else result + reduced
    return result * norm_factor


def solution(mesh):
    in_specs = (
        P(("groups", "aux"), "bas", None, None, None),
        P(("groups", "bas"), None),
        P(("groups", "bas"), None),
        P("groups", None),
        P("groups", None),
    )
    out_specs = P(("groups", "bas"), "aux")
    return jax.shard_map(
        on_device, mesh=mesh, in_specs=in_specs, out_specs=out_specs, check_vma=False
    )
```

profile of v0, /device:TPU:9, one launch (start us, length us, event | category | flops | bytes accessed | tf_op | source)
XLA Modules:
  0.0 223.2 jit_solution(2286100574240368245)
XLA Ops:
  6.5 0.8 convert_element_type.15
  7.4 0.1 copy.16
  7.5 0.8 fusion.21
  8.2 0.7 compare_select_fusion
  8.9 0.1 copy.14
  9.0 0.1 reshape.83
  9.1 0.9 gather_fusion
  10.1 0.1 copy_bitcast_fusion.1
  10.2 1.7 gather_fusion.1
  11.8 6.1 %fusion.8 = bf16[128,8,8,128]{0,3,1,2:T(8,128)(2,1)S(1)} fusion(bf16[8,8,4,128,128]{4,3,2,1,0:T(8,128)(2,1)} %param.5, bf16[8,4,128,128]{3,2,1,0:T(8,128)(2,1)} %bitcast.63, bf16[8,4]{1,0:T(8,128)(2,1)S(1)} %copy.16), kind=kOutput, calls=%fused_computation.11 | convolution fusion | flops 1076887552 | bytes 11534400 | tf_op jit(solution)/shard_map/ptkxy,itky->iptx/dot_general | solution.py:22
  18.0 1.4 copy.18
  19.4 3.9 %copy.19 = bf16[128,8,1024]{2,0,1:T(8,128)(2,1)} copy(bf16[128,8,1024]{0,2,1:T(8,128)(2,1)} %bitcast.58) | data formatting | bytes 4194304 | tf_op jit(solution)/shard_map/reshape | solution.py:25
  23.4 0.9 gather_fusion.2
  24.3 0.1 copy_bitcast_fusion
  24.5 1.7 gather_fusion.3
  26.1 6.1 %fusion.11 = bf16[128,8,8,128]{0,3,1,2:T(8,128)(2,1)S(1)} fusion(bf16[8,8,4,128,128]{4,3,2,1,0:T(8,128)(2,1)} %param.5, bf16[8,4,128,128]{3,2,1,0:T(8,128)(2,1)} %bitcast.62, bf16[8,4]{1,0:T(8,128)(2,1)S(1)} %copy.16), kind=kOutput, calls=%fused_computation.12 | convolution fusion | flops 1076887552 | bytes 11534400 | tf_op jit(solution)/shard_map/ptkxy,itky->iptx/dot_general | solution.py:22
  32.3 1.5 copy.22
  33.7 4.0 %copy.23 = bf16[128,8,1024]{2,0,1:T(8,128)(2,1)} copy(bf16[128,8,1024]{0,2,1:T(8,128)(2,1)} %bitcast.60) | data formatting | bytes 4194304 | tf_op jit(solution)/shard_map/reshape | solution.py:25
  37.8 1.2 all-gather.3.cloned.1.call-done
  39.1 8.9 %fusion.22 = f32[1024,2048,1]{1,0,2:T(8,128)} fusion(bf16[128,8,1024]{0,2,1:T(8,128)(2,1)} %bitcast.59, bf16[128,8,2048]{2,0,1:T(8,128)(2,1)} %all-gather.3.cloned.1.call-done), kind=kOutput, calls=%fused_computation.30 | convolution fusion | flops 4294967296 | bytes 14680064 | tf_op jit(solution)/shard_map/dot_general | solution.py:28
  47.9 7.5 %all-gather.5.cloned.1.call-done = bf16[128,8,2048]{2,0,1:T(8,128)(2,1)} async-done(((bf16[128,8,1024]{2,0,1:T(8,128)(2,1)}), bf16[128,8,2048]{2,0,1:T(8,128)(2,1)}) %all-gather.5.cloned.1.call-update) | async-done | bytes 4194320 | tf_op jit(solution)/shard_map/all_gather | solution.py:30
  55.5 10.4 %bitcast_add_fusion = f32[1024,2048]{1,0:T(8,128)} fusion(f32[1024,2048,1]{1,0,2:T(8,128)} %fusion.22, bf16[128,8,1024]{0,2,1:T(8,128)(2,1)} %bitcast.61, bf16[128,8,2048]{2,0,1:T(8,128)(2,1)} %all-gather.5.cloned.1.call-done), kind=kOutput, calls=%fused_computation.4 | convolution fusion | flops 4297064448 | bytes 23068672 | tf_op jit(solution)/shard_map/dot_general | solution.py:28
  65.9 148.5 %reduce-scatter.2.cloned.1.call-done = f32[1024,256]{1,0:T(8,128)} async-done(((f32[1024,2048]{1,0:T(8,128)}), f32[1024,256]{1,0:T(8,128)}) %reduce-scatter.2.cloned.1.call-update) | async-done | bytes 1048592 | tf_op jit(solution)/shard_map/reduce_scatter | solution.py:34
  214.4 2.3 %broadcast_multiply_fusion = f32[1024,256]{1,0:T(8,128)} fusion(f32[1024,256]{1,0:T(8,128)} %reduce-scatter.2.cloned.1.call-done), kind=kLoop, calls=%fused_computation.21 | loop fusion | flops 262144 | bytes 2097152 | tf_op jit(solution)/shard_map/mul | solution.py:36
  (10 shorter events, 0.2 us)
Async XLA Ops:
  6.5 2.6 %copy-start = (bf16[512,2048]{1,0:T(8,128)(2,1)S(1)}, bf16[512,2048]{1,0:T(8,128)(2,1)}, u32[]{:S(2)}) copy-start(bf16[512,2048]{1,0:T(8,128)(2,1)} %param.8) | copy-start | bytes 6291460
  6.5 32.5 %all-gather.3.cloned.1.call-start = ((), (), s32[]{:S(2)}) async-start(), calls=%async_computation.1 | async-start | bytes 6291456 | tf_op jit(solution)/shard_map/all_gather | solution.py:30
  23.3 32.1 %all-gather.5.cloned.1.call-start = ((), (), s32[]{:S(2)}) async-start(), calls=%async_computation.2 | async-start | bytes 6291456 | tf_op jit(solution)/shard_map/all_gather | solution.py:30
  37.8 176.7 %reduce-scatter.2.cloned.1.call-start = ((), (), s32[]{:S(2)}) async-start(), calls=%async_computation.3 | async-start | bytes 9437184 | tf_op jit(solution)/shard_map/reduce_scatter | solution.py:34
Sparse Core Ops, SparseCore 0:
  23.5 15.5 all-gather.2
  40.6 14.8 all-gather.4
  66.1 148.3 reduce-scatter.1
where the time goes:
time: 227 us; the launch traced here: 223 us
  waiting for transfers between devices  157 us (69%)
  matrix products  31.6 us (14%)
  local copies, waits for them, and re-layouts  16.5 us (7%)
  between operations  13.2 us (6%)
  other arithmetic  4.55 us (2%)
    reduce_scatter x1, waiting for transfers between devices, on_device(): lax.psum_scatter(partial_value, 'aux', scatter_dimension=1, tiled=True)  149 us
    dot_general x2, matrix products, on_device(): lax.dot_general(source, lax.all_gather(source, 'bas', axis=2, tiled=True)...  19.3 us
    dot_general x2, matrix products, on_device(): jnp.einsum('ptkxy,itky->iptx', factors, picked, preferred_element_type=jn...  12.3 us
    all_gather x2, waiting for transfers between devices, on_device(): lax.all_gather(source, 'bas', axis=2, tiled=True)  8.77 us
    reshape x2, local copies, waits for them, and re-layouts, on_device(): half_done.astype(jnp.bfloat16)  7.92 us
  transfers between devices with their start and end apart: 3, of which 3 were waited for; matrix products, arithmetic and copies ran while one was open for 10% of the time, Pallas kernels for 0%

commit v1 on v0

v1 whole, which is shorter than its diff:
```python
import functools
import math

import jax
import jax.numpy as jnp
from jax import lax
from jax.experimental import pallas as pl
from jax.experimental.pallas import tpu as pltpu
from jax.sharding import PartitionSpec as P

MESH = pl.DeviceIdType.MESH
LAST = (((1,), (1,)), ((), ()))
ORDER = [sum(d * 4**s for s, d in enumerate(row)) for row in ((1, 3, 2, 0), (0, 3, 2, 1), (0, 3, 1, 2), (0, 1, 2, 3))]


def half_kernel(cols_ref, live_ref, rows_ref, coef_ref, fac_ref, out_ref, picked):
    t = pl.program_id(0)
    aux, _, slots, tile, _ = fac_ref.shape
    batches, occ = rows_ref.shape
    norb = coef_ref.shape[0]

    @pl.when(t == 0)
    def _():
        ids = lax.broadcasted_iota(jnp.int32, (norb, occ), 0)
        for b in range(batches):
            onehot = (ids == rows_ref[b : b + 1, :]).astype(jnp.float32).T.astype(jnp.bfloat16)
            picked[b * occ : (b + 1) * occ, :] = jnp.dot(
                onehot, coef_ref[...], preferred_element_type=jnp.float32
            ).astype(jnp.bfloat16)

    parts = []
    for k in range(slots):
        block = picked[:, pl.ds(pl.multiple_of(cols_ref[t, k] * tile, tile), tile)]
        parts.append(block * live_ref[t, k].astype(jnp.float32).astype(jnp.bfloat16))
    weights = jnp.concatenate(parts, axis=1)
    width = batches * occ
    for p in range(aux):
        lhs = jnp.concatenate([fac_ref[p, 0, k] for k in range(slots)], axis=1)
        out_ref[:, p * width : (p + 1) * width] = lax.dot_general(
            lhs, weights, LAST, preferred_element_type=jnp.float32
        ).astype(jnp.bfloat16)


def half_transformed(factors, tile_cols, tile_live, coefficients, batch_rows):
    aux, tiles, slots, tile, _ = factors.shape
    batches, occ = batch_rows.shape
    depth = aux * batches * occ
    smem = pl.BlockSpec(memory_space=pltpu.SMEM)
    return pl.pallas_call(
        half_kernel,
        grid=(tiles,),
        out_shape=jax.ShapeDtypeStruct((tiles * tile, depth), jnp.bfloat16),
        in_specs=[
            smem,
            smem,
            pl.BlockSpec(batch_rows.shape, lambda t: (0, 0)),
            pl.BlockSpec(coefficients.shape, lambda t: (0, 0)),
            pl.BlockSpec((aux, 1, slots, tile, tile), lambda t: (0, t, 0, 0, 0)),
        ],
        out_specs=pl.BlockSpec((tile, depth), lambda t: (t, 0)),
        scratch_shapes=[pltpu.VMEM((batches * occ, coefficients.shape[1]), jnp.bfloat16)],
        compiler_params=pltpu.CompilerParams(vmem_limit_bytes=40 * 2**20),
        cost_estimate=pl.CostEstimate(flops=2 * factors.size * batches * occ, bytes_accessed=factors.size * 2, transcendentals=0),
    )(tile_cols, tile_live, batch_rows, coefficients, factors)


def exchange_kernel(
    norm, half_ref, out_ref, h, ytx, yrx, acc, ztx, zrx, ftx, frx,
    own_sem, h_send, h_recv, y_send, y_recv, z_send, z_recv, f_send, f_recv,
):
    g, aux, b = lax.axis_index("groups"), lax.axis_index("aux"), lax.axis_index("bas")
    y, z = lax.rem(aux, 2), aux // 2
    rows = half_ref.shape[0]
    w = jnp.where(b == 0, z, 3 - z)
    packed = jnp.where(w == 0, ORDER[0], jnp.where(w == 1, ORDER[1], jnp.where(w == 2, ORDER[2], ORDER[3])))

    def dest(s):
        scale = jnp.where(s == 0, 1, jnp.where(s == 1, 4, jnp.where(s == 2, 16, 64)))
        wd = lax.rem(packed // scale, 4)
        return jnp.where(b == 0, wd, 3 - wd)

    barrier = pltpu.get_barrier_semaphore()
    for step in range(1, 16):
        other = lax.rem(aux * 2 + b + step, 16)
        pl.semaphore_signal(barrier, inc=1, device_id=(g, other // 2, lax.rem(other, 2)), device_id_type=MESH)

    mine = pl.ds(pl.multiple_of(b * rows, 1024), rows)
    own_copy = pltpu.make_async_copy(half_ref, h.at[mine], own_sem)
    own_copy.start()
    pl.semaphore_wait(barrier, 15)
    swap = pltpu.make_async_remote_copy(
        src_ref=half_ref, dst_ref=h.at[mine], send_sem=h_send, recv_sem=h_recv,
        device_id=(g, aux, 1 - b), device_id_type=MESH,
    )
    swap.start()

    def piece(o, slot):
        r = jnp.where(slot == 4, o, b * 4 + slot)
        upper = jnp.where(slot == 4, 1, jnp.where(o > r, 1, 0))
        hi, lo = jnp.maximum(o, r), jnp.minimum(o, r)
        left = h[pl.ds(pl.multiple_of(hi * 256 + upper * 128, 128), 128), :]
        right = h[pl.ds(pl.multiple_of(lo * 256, 256), 256), :]
        return lax.dot_general(left, right, LAST, preferred_element_type=jnp.float32)

    diagonal = lax.broadcasted_iota(jnp.int32, (128, 128), 0) == lax.broadcasted_iota(jnp.int32, (128, 128), 1)
    row_ids = lax.broadcasted_iota(jnp.int32, (128, 128), 0)

    def lost(block):
        rest = block - block.astype(jnp.bfloat16).astype(jnp.float32)
        return jnp.sum(jnp.where(diagonal, rest, 0.0), axis=0, keepdims=True)

    def lost_rows(first, second):
        return jnp.where(row_ids == 0, lost(first), jnp.where(row_ids == 1, lost(second), 0.0))

    CHUNKS = ((0, 256), (256, 256), (512, 128))

    def extra(zd):
        return zd // 2 == b

    def each_chunk(zd, body):
        body(0)
        body(1)

        @pl.when(extra(zd))
        def _():
            body(2)

    def y_copy(s, c):
        at, size = CHUNKS[c]
        return pltpu.make_async_remote_copy(
            src_ref=ytx.at[s, pl.ds(at, size)], dst_ref=yrx.at[s, pl.ds(at, size)],
            send_sem=y_send.at[s, c], recv_sem=y_recv.at[s, c],
            device_id=(g, z * 2 + 1 - y, b), device_id_type=MESH,
        )

    def z_copy(zd, up, c, to):
        at, size = CHUNKS[c]
        return pltpu.make_async_remote_copy(
            src_ref=ztx.at[zd, pl.ds(at, size)], dst_ref=zrx.at[up, zd, pl.ds(at, size)],
            send_sem=z_send.at[zd, c], recv_sem=z_recv.at[up, zd, c],
            device_id=(g, to * 2 + y, b), device_id_type=MESH,
        )

    own_copy.wait()

    def y_step(s, carry):
        @pl.when(s == 1)
        def _():
            swap.wait()

        zd = dest(s)
        o = zd * 2 + 1 - y

        def chunk(c):
            def one(slot, carry):
                ytx[s, pl.ds(pl.multiple_of(slot * 128, 128), 128), :] = piece(o, slot).astype(jnp.bfloat16)
                return carry

            at, size = CHUNKS[c]
            if c < 2:
                lax.fori_loop(at // 128, (at + size) // 128, one, 0)
            else:
                first, second = piece(o, lax.rem(o, 4))[:, :128], piece(o, 4)[:, 128:]
                ytx[s, 512:640, 0:128] = lost_rows(first, second).astype(jnp.bfloat16)
                ytx[s, 512:640, 128:256] = second.astype(jnp.bfloat16)
            y_copy(s, c).start()

        each_chunk(zd, chunk)
        return carry

    lax.fori_loop(0, 4, y_step, 0)

    def own_step(s, carry):
        zd = dest(s)
        o = zd * 2 + y

        def one(slot, carry):
            acc[s, pl.ds(pl.multiple_of(slot * 128, 128), 128), :] = piece(o, slot)
            return carry

        lax.fori_loop(0, jnp.where(extra(zd), 5, 4), one, 0)
        acc[s, 512:640, 0:128] = jnp.zeros((128, 128), jnp.float32)
        return carry

    lax.fori_loop(0, 4, own_step, 0)

    def add(s, c, ref):
        at, size = CHUNKS[c]
        acc[s, pl.ds(at, size), :] += ref[pl.ds(at, size), :].astype(jnp.float32)

    def chain_step(s, carry):
        zd = dest(s)
        up = jnp.where(zd > z, 0, 1)
        before = jnp.where(zd > z, z - 1, z + 1)
        has_before = jnp.logical_and(before >= 0, before < 4)

        def chunk(c):
            at, size = CHUNKS[c]
            y_copy(s, c).wait_recv()
            add(s, c, yrx.at[s])

            @pl.when(has_before)
            def _():
                z_copy(zd, up, c, before).wait_recv()
                add(s, c, zrx.at[up, zd])

            if c < 2:
                ztx[zd, pl.ds(at, size), :] = acc[s, pl.ds(at, size), :].astype(jnp.bfloat16)
            else:
                own_slot = pl.multiple_of(lax.rem(zd * 2 + y, 4) * 128, 128)
                first, second = acc[s, pl.ds(own_slot, 128), 0:128], acc[s, 512:640, 128:256]
                rest = acc[s, 512:640, 0:128] + lost_rows(first, second)
                ztx[zd, 512:640, 0:128] = rest.astype(jnp.bfloat16)
                ztx[zd, 512:640, 128:256] = second.astype(jnp.bfloat16)
            z_copy(zd, up, c, jnp.where(zd > z, z + 1, z - 1)).start()

        each_chunk(zd, chunk)
        return carry

    lax.fori_loop(0, 3, chain_step, 0)

    def f_copy(j, to, to_core, slot_at):
        return pltpu.make_async_remote_copy(
            src_ref=ftx.at[j], dst_ref=frx.at[slot_at], send_sem=f_send.at[j], recv_sem=f_recv.at[slot_at],
            device_id=(g, to, to_core), device_id_type=MESH,
        )

    def last(c):
        at, size = CHUNKS[c]
        y_copy(3, c).wait_recv()
        add(3, c, yrx.at[3])

        @pl.when(z > 0)
        def _():
            z_copy(z, 0, c, z).wait_recv()
            add(3, c, zrx.at[0, z])

        @pl.when(z < 3)
        def _():
            z_copy(z, 1, c, z).wait_recv()
            add(3, c, zrx.at[1, z])

        if c < 2:
            for j in (2 * c, 2 * c + 1):
                r = b * 4 + j

                @pl.when(r != aux)
                def _():
                    ftx[j] = acc[3, pl.ds(j * 128, 128), :].astype(jnp.bfloat16)
                    f_copy(j, r, aux // 4, lax.rem(aux, 4)).start()

    each_chunk(z, last)

    for j in range(4):
        r = b * 4 + j
        low, high = j * 256, j * 256 + 128

        @pl.when(r == aux)
        def _():
            for side in range(2):
                rest = jnp.where(diagonal, acc[3, 512 + side : 513 + side, 0:128], 0.0)
                source = acc[3, j * 128 : j * 128 + 128, 0:128] if side == 0 else acc[3, 512:640, 128:256]
                at = low + side * 128
                out_ref[at : at + 128, side * 128 : side * 128 + 128] = (source + rest) * norm
            corner = acc[3, j * 128 : j * 128 + 128, 128:256] * norm
            out_ref[low:high, 128:256] = corner
            out_ref[high : high + 128, 0:128] = corner.T

        @pl.when(r > aux)
        def _():
            out_ref[low:high, :] = acc[3, pl.ds(j * 128, 128), :] * norm

        @pl.when(r < aux)
        def _():
            out_ref[low : low + 256, 128:256] = (acc[3, pl.ds(j * 128, 128), :] * norm).T

    for j in range(4):
        r = b * 4 + j
        low, high = j * 256, j * 256 + 128

        @pl.when(r != aux)
        def _():
            f_copy(j, r, aux // 4, j).wait_recv()

        @pl.when(r > aux)
        def _():
            out_ref[high : high + 128, :] = frx[j].astype(jnp.float32) * norm

        @pl.when(r < aux)
        def _():
            out_ref[low : low + 256, 0:128] = (frx[j].astype(jnp.float32) * norm).T

    def drain(s, carry):
        zd = dest(s)
        each_chunk(zd, lambda c: y_copy(s, c).wait_send())

        @pl.when(zd != z)
        def _():
            each_chunk(zd, lambda c: z_copy(zd, 0, c, z).wait_send())

        return carry

    lax.fori_loop(0, 4, drain, 0)
    for j in range(4):
        r = b * 4 + j

        @pl.when(r != aux)
        def _():
            f_copy(j, r, aux // 4, j).wait_send()


def exchange(half, norm):
    rows, depth = half.shape
    dma = pltpu.SemaphoreType.DMA
    bf16, f32 = jnp.bfloat16, jnp.float32
    return pl.pallas_call(
        functools.partial(exchange_kernel, norm),
        out_shape=jax.ShapeDtypeStruct((rows, 256), f32),
        in_specs=[pl.BlockSpec(memory_space=pl.ANY)],
        out_specs=pl.BlockSpec(memory_space=pltpu.VMEM),
        scratch_shapes=[
            pltpu.VMEM((2 * rows, depth), bf16),
            pltpu.VMEM((4, 640, 256), bf16),
            pltpu.VMEM((4, 640, 256), bf16),
            pltpu.VMEM((4, 640, 256), f32),
            pltpu.VMEM((4, 640, 256), bf16),
            pltpu.VMEM((2, 4, 640, 256), bf16),
            pltpu.VMEM((4, 128, 256), bf16),
            pltpu.VMEM((4, 128, 256), bf16),
            dma, dma, dma, dma((4, 3)), dma((4, 3)), dma((4, 3)), dma((2, 4, 3)), dma((4,)), dma((4,)),
        ],
        compiler_params=pltpu.CompilerParams(
            collective_id=0, has_side_effects=True, vmem_limit_bytes=48 * 2**20
        ),
        cost_estimate=pl.CostEstimate(flops=2 * rows * rows * depth, bytes_accessed=half.size * 2, transcendentals=0),
    )(half)


def general(half, norm):
    everyone = lax.all_gather(half, "bas", axis=0, tiled=True)
    partial_value = lax.dot_general(half, everyone, LAST, preferred_element_type=jnp.float32)
    return lax.psum_scatter(partial_value, "aux", scatter_dimension=1, tiled=True) * norm


def on_device(factors, tile_cols, tile_live, coefficients, batch_rows):
    members = lax.axis_size("aux")
    norm = 1.0 / math.sqrt(factors.shape[0] * members * batch_rows.size)
    half = half_transformed(factors, tile_cols, tile_live, coefficients, batch_rows)
    columns = coefficients.shape[1] // members
    if members == 8 and lax.axis_size("bas") == 2 and columns == 256:
        return exchange(half, norm)
    return general(half, norm)


def solution(mesh):
    in_specs = (
        P(("groups", "aux"), "bas", None, None, None),
        P(("groups", "bas"), None),
        P(("groups", "bas"), None),
        P("groups", None),
        P("groups", None),
    )
    out_specs = P(("groups", "bas"), "aux")
    return jax.shard_map(
        on_device, mesh=mesh, in_specs=in_specs, out_specs=out_specs, check_vma=False
    )
```

time: 227 us -> 75.5 us (0.33); the launches traced: 223 us -> 74.5 us
  waiting for transfers between devices: 157 us -> 0 us
  Pallas kernels: 0 us -> 69.7 us
  matrix products: 31.6 us -> 0 us
  between operations: 13.2 us -> 0.02 us
  local copies, waits for them, and re-layouts: 16.5 us -> 4.75 us
  other arithmetic: 4.55 us -> 0 us
    reduce_scatter x1 -> x0, waiting for transfers between devices: 149 us -> none  [on_device(): lax.psum_scatter(partial_value, 'aux', scatter_dimension=1, tiled=True)]
    pallas_call x0 -> x2, Pallas kernels: none -> 69.7 us  [the longest x1 59.6 us: exchange(): pl.pallas_call(functools.partial(exchange_kernel, norm), out_shape=jax.Sh...]
    dot_general x4 -> x0, matrix products: 31.6 us -> none  [the longest x2 19.3 us: on_device(): lax.dot_general(source, lax.all_gather(source, 'bas', axis=2, tiled=True)...]
    all_gather x2 -> x0, waiting for transfers between devices: 8.77 us -> none  [on_device(): lax.all_gather(source, 'bas', axis=2, tiled=True)]
    reshape x4 -> x0, local copies, waits for them, and re-layouts: 8.18 us -> none  [the longest x2 7.92 us: on_device(): half_done.astype(jnp.bfloat16)]
    gather x4 -> x0, local copies, waits for them, and re-layouts: 5.17 us -> none  [the longest x2 3.3 us: on_device(): picked = orbital_rows[:, tile_cols, :] * live_mask[None, :, :, None]]
    unnamed x2 -> x7, local copies, waits for them, and re-layouts: 0.01 us -> 4.75 us
    convert_element_type x3 -> x0, local copies, waits for them, and re-layouts: 3.02 us -> none  [the longest x2 2.93 us: on_device(): half_done.astype(jnp.bfloat16)]
  transfers between devices with their start and end apart: 3 -> 0, of which waited for: 3 -> 0; matrix products, arithmetic and copies ran while one was open for 10% -> 0% of each run, Pallas kernels for 0% -> 0%
where the time goes in v1:
time: 75.5 us; the launch traced here: 74.5 us
  Pallas kernels  69.7 us (92%)
  local copies, waits for them, and re-layouts  4.75 us (6%)
    pallas_call x1, Pallas kernels, exchange(): pl.pallas_call(functools.partial(exchange_kernel, norm), out_shape=jax.Sh...  59.6 us
    pallas_call x1, Pallas kernels, half_transformed(): pl.pallas_call(half_kernel, grid=(tiles,), out_shape=jax.ShapeDtypeStruct...  10.1 us
    unnamed x7, local copies, waits for them, and re-layouts  4.75 us

profile of v1, /device:TPU:9, one launch (start us, length us, event | category | flops | bytes accessed | tf_op | source)
XLA Modules:
  0.0 74.5 jit_solution(5024617167984275185)
XLA Ops:
  0.0 0.8 %copy.6.cols_ref = s32[8,4]{1,0:T(8,128)S(1)} copy(s32[8,4]{0,1:T(4,128)} %param.6) | data formatting | bytes 256 | tf_op args[1]
  0.8 0.8 %copy.7.live_ref = s32[8,4]{1,0:T(8,128)S(1)} copy(s32[8,4]{0,1:T(4,128)} %param.7) | data formatting | bytes 256 | tf_op args[2]
  1.5 0.0 copy-start
  1.5 1.6 %copy-done = bf16[512,2048]{1,0:T(8,128)(2,1)S(1)} copy-done((bf16[512,2048]{1,0:T(8,128)(2,1)S(1)}, bf16[512,2048]{1,0:T(8,128)(2,1)}, u32[]{:S(2)}) %copy-start) | copy-done | bytes 2097176
  3.1 0.0 copy-start.1
  3.1 0.7 copy-done.1
  3.8 10.1 %shard_map.55.half_ref = bf16[1024,2048]{1,0:T(8,128)(2,1)S(1)} custom-call(s32[8,4]{1,0:T(8,128)S(1)} %copy.6.cols_ref, s32[8,4]{1,0:T(8,128)S(1)} %copy.7.live_ref, s32[2,128]{1,0:T(2,128)S(1)} %copy-done.1, bf16[512,2048]{1,0:T(8,128)(2,1)S(1)} %copy-done, bf16[8,8,4,128,128]{4,3,2,1,0:T(8,128)(2,1)} %fac_ref.1), custom_call_target="tpu_custom_call" | custom-call | flops 2147483648 | bytes 8388608 | tf_op jit(solution)/shard_map/pallas_call | solution.py:49
  13.9 59.6 %shard_map.56 = f32[1024,256]{1,0:T(8,128)S(1)} custom-call(bf16[1024,2048]{1,0:T(8,128)(2,1)S(1)} %shard_map.55.half_ref), custom_call_target="tpu_custom_call" | custom-call | flops 4294967296 | bytes 4194304 | tf_op jit(solution)/shard_map/pallas_call | solution.py:316
  73.5 1.0 %copy.9 = f32[1024,256]{1,0:T(8,128)} copy(f32[1024,256]{1,0:T(8,128)S(1)} %shard_map.56) | data formatting | bytes 2097152
Async XLA Ops:
  1.5 1.6 %copy-start = (bf16[512,2048]{1,0:T(8,128)(2,1)S(1)}, bf16[512,2048]{1,0:T(8,128)(2,1)}, u32[]{:S(2)}) copy-start(bf16[512,2048]{1,0:T(8,128)(2,1)} %coef_ref.1) | copy-start | bytes 6291460
  3.1 0.7 copy-start.1

commit v2 on v1

--- a/solution.py
+++ b/solution.py
@@ -30,15 +30,14 @@
 
     parts = []
     for k in range(slots):
-        block = picked[:, pl.ds(pl.multiple_of(cols_ref[t, k] * tile, tile), tile)]
-        parts.append(block * live_ref[t, k].astype(jnp.float32).astype(jnp.bfloat16))
+        block = picked[:, pl.ds(pl.multiple_of(cols_ref[k, t] * tile, tile), tile)]
+        parts.append(block * live_ref[k, t].astype(jnp.float32).astype(jnp.bfloat16))
     weights = jnp.concatenate(parts, axis=1)
     width = batches * occ
+    lhs = jnp.concatenate([fac_ref[:, 0, k].reshape(aux * tile, tile) for k in range(slots)], axis=1)
+    half = lax.dot_general(lhs, weights, LAST, preferred_element_type=jnp.float32).astype(jnp.bfloat16)
     for p in range(aux):
-        lhs = jnp.concatenate([fac_ref[p, 0, k] for k in range(slots)], axis=1)
-        out_ref[:, p * width : (p + 1) * width] = lax.dot_general(
-            lhs, weights, LAST, preferred_element_type=jnp.float32
-        ).astype(jnp.bfloat16)
+        out_ref[:, p * width : (p + 1) * width] = half[p * tile : (p + 1) * tile]
 
 
 def half_transformed(factors, tile_cols, tile_live, coefficients, batch_rows):
@@ -61,11 +60,11 @@
         scratch_shapes=[pltpu.VMEM((batches * occ, coefficients.shape[1]), jnp.bfloat16)],
         compiler_params=pltpu.CompilerParams(vmem_limit_bytes=40 * 2**20),
         cost_estimate=pl.CostEstimate(flops=2 * factors.size * batches * occ, bytes_accessed=factors.size * 2, transcendentals=0),
-    )(tile_cols, tile_live, batch_rows, coefficients, factors)
+    )(tile_cols.T, tile_live.T, batch_rows, coefficients, factors)
 
 
 def exchange_kernel(
-    norm, half_ref, out_ref, h, ytx, yrx, acc, ztx, zrx, ftx, frx,
+    norm, half_ref, out_ref, h, tall, ytx, yrx, acc, ztx, zrx, ftx, frx,
     own_sem, h_send, h_recv, y_send, y_recv, z_send, z_recv, f_send, f_recv,
 ):
     g, aux, b = lax.axis_index("groups"), lax.axis_index("aux"), lax.axis_index("bas")
@@ -94,14 +93,6 @@
     )
     swap.start()
 
-    def piece(o, slot):
-        r = jnp.where(slot == 4, o, b * 4 + slot)
-        upper = jnp.where(slot == 4, 1, jnp.where(o > r, 1, 0))
-        hi, lo = jnp.maximum(o, r), jnp.minimum(o, r)
-        left = h[pl.ds(pl.multiple_of(hi * 256 + upper * 128, 128), 128), :]
-        right = h[pl.ds(pl.multiple_of(lo * 256, 256), 256), :]
-        return lax.dot_general(left, right, LAST, preferred_element_type=jnp.float32)
-
     diagonal = lax.broadcasted_iota(jnp.int32, (128, 128), 0) == lax.broadcasted_iota(jnp.int32, (128, 128), 1)
     row_ids = lax.broadcasted_iota(jnp.int32, (128, 128), 0)
 
@@ -143,46 +134,82 @@
 
     own_copy.wait()
 
-    def y_step(s, carry):
+    def top(r):
+        return h[pl.ds(pl.multiple_of(r * 256, 256), 128), :]
+
+    def bottom(r):
+        return h[pl.ds(pl.multiple_of(r * 256 + 128, 128), 128), :]
+
+    def block(r):
+        return h[pl.ds(pl.multiple_of(r * 256, 256), 256), :]
+
+    def dot(left, right):
+        return lax.dot_general(left, right, LAST, preferred_element_type=jnp.float32)
+
+    def compute_step(s, carry):
         @pl.when(s == 1)
         def _():
             swap.wait()
 
         zd = dest(s)
-        o = zd * 2 + 1 - y
-
-        def chunk(c):
+        theirs, ours = zd * 2 + 1 - y, zd * 2 + y
+        starts = [b * 4 + j for j in range(4)]
+
+        def smaller(o, store):
             def one(slot, carry):
-                ytx[s, pl.ds(pl.multiple_of(slot * 128, 128), 128), :] = piece(o, slot).astype(jnp.bfloat16)
+                store(pl.ds(pl.multiple_of(slot * 128, 128), 128), dot(bottom(o), block(b * 4 + slot)))
                 return carry
 
-            at, size = CHUNKS[c]
-            if c < 2:
-                lax.fori_loop(at // 128, (at + size) // 128, one, 0)
-            else:
-                first, second = piece(o, lax.rem(o, 4))[:, :128], piece(o, 4)[:, 128:]
-                ytx[s, 512:640, 0:128] = lost_rows(first, second).astype(jnp.bfloat16)
-                ytx[s, 512:640, 128:256] = second.astype(jnp.bfloat16)
-            y_copy(s, c).start()
-
-        each_chunk(zd, chunk)
+            lax.fori_loop(0, lax.rem(o, 4), one, 0)
+
+        def store_theirs(at, value):
+            ytx[s, at, :] = value.astype(jnp.bfloat16)
+
+        def store_ours(at, value):
+            acc[s, at, :] = value
+
+        @pl.when(extra(zd))
+        def _():
+            full = dot(jnp.concatenate([top(r) for r in starts] + [bottom(theirs)], axis=0), block(theirs))
+            tall[...] = full
+            store_theirs(pl.ds(0, 512), full[:512])
+            first = tall[pl.ds(pl.multiple_of(lax.rem(theirs, 4) * 128, 128), 128), 0:128]
+            second = full[512:, 128:]
+            ytx[s, 512:640, 0:128] = lost_rows(first, second).astype(jnp.bfloat16)
+            ytx[s, 512:640, 128:256] = second.astype(jnp.bfloat16)
+            smaller(theirs, store_theirs)
+            for c in range(3):
+                y_copy(s, c).start()
+            full = dot(jnp.concatenate([top(r) for r in starts] + [bottom(ours)], axis=0), block(ours))
+            store_ours(pl.ds(0, 512), full[:512])
+            acc[s, 512:640, 0:128] = jnp.zeros((128, 128), jnp.float32)
+            acc[s, 512:640, 128:256] = full[512:, 128:]
+            smaller(ours, store_ours)
+
+        @pl.when(jnp.logical_and(jnp.logical_not(extra(zd)), b == 1))
+        def _():
+            left = jnp.concatenate([top(r) for r in starts], axis=0)
+            store_theirs(pl.ds(0, 512), dot(left, block(theirs)))
+            for c in range(2):
+                y_copy(s, c).start()
+            store_ours(pl.ds(0, 512), dot(left, block(ours)))
+
+        @pl.when(jnp.logical_and(jnp.logical_not(extra(zd)), b == 0))
+        def _():
+            def one(slot, carry):
+                both = dot(jnp.concatenate([bottom(theirs), bottom(ours)], axis=0), block(slot))
+                at = pl.ds(pl.multiple_of(slot * 128, 128), 128)
+                store_theirs(at, both[:128])
+                store_ours(at, both[128:])
+                return carry
+
+            for c in range(2):
+                lax.fori_loop(2 * c, 2 * c + 2, one, 0)
+                y_copy(s, c).start()
+
         return carry
 
-    lax.fori_loop(0, 4, y_step, 0)
-
-    def own_step(s, carry):
-        zd = dest(s)
-        o = zd * 2 + y
-
-        def one(slot, carry):
-            acc[s, pl.ds(pl.multiple_of(slot * 128, 128), 128), :] = piece(o, slot)
-            return carry
-
-        lax.fori_loop(0, jnp.where(extra(zd), 5, 4), one, 0)
-        acc[s, 512:640, 0:128] = jnp.zeros((128, 128), jnp.float32)
-        return carry
-
-    lax.fori_loop(0, 4, own_step, 0)
+    lax.fori_loop(0, 4, compute_step, 0)
 
     def add(s, c, ref):
         at, size = CHUNKS[c]
@@ -320,6 +347,7 @@
         out_specs=pl.BlockSpec(memory_space=pltpu.VMEM),
         scratch_shapes=[
             pltpu.VMEM((2 * rows, depth), bf16),
+            pltpu.VMEM((640, 256), f32),
             pltpu.VMEM((4, 640, 256), bf16),
             pltpu.VMEM((4, 640, 256), bf16),
             pltpu.VMEM((4, 640, 256), f32),

time: 75.5 us -> 64.8 us (0.86)
  Pallas kernels: 69.7 us -> 59 us
    pallas_call x1, Pallas kernels: 59.6 us -> 50.4 us  [exchange(): pl.pallas_call(functools.partial(exchange_kernel, norm), out_shape=jax.Sh...]
    pallas_call x1, Pallas kernels: 10.1 us -> 8.65 us  [half_transformed(): pl.pallas_call(half_kernel, grid=(tiles,), out_shape=jax.ShapeDtypeStruct...]
    unnamed x7 -> x9, local copies, waits for them, and re-layouts: 4.75 us -> 4.6 us
where the time goes in v2:
time: 64.8 us; the launch traced here: 63.6 us
  Pallas kernels  59 us (91%)
  local copies, waits for them, and re-layouts  4.6 us (7%)
    pallas_call x1, Pallas kernels, exchange(): pl.pallas_call(functools.partial(exchange_kernel, norm), out_shape=jax.Sh...  50.4 us
    pallas_call x1, Pallas kernels, half_transformed(): pl.pallas_call(half_kernel, grid=(tiles,), out_shape=jax.ShapeDtypeStruct...  8.65 us
    unnamed x9, local copies, waits for them, and re-layouts  4.6 us

profile of v2, /device:TPU:9, one launch (start us, length us, event | category | flops | bytes accessed | tf_op | source)
XLA Modules:
  0.0 63.6 jit_solution(5373125329954293178)
XLA Ops:
  0.0 0.0 copy-start
  0.0 1.6 %copy-done = bf16[512,2048]{1,0:T(8,128)(2,1)S(1)} copy-done((bf16[512,2048]{1,0:T(8,128)(2,1)S(1)}, bf16[512,2048]{1,0:T(8,128)(2,1)}, u32[]{:S(2)}) %copy-start) | copy-done | bytes 2097176
  1.6 0.0 copy-start.1
  1.6 0.7 %copy-done.1 = s32[8,4]{0,1:T(4,128)S(1)} copy-done((s32[8,4]{0,1:T(4,128)S(1)}, s32[8,4]{0,1:T(4,128)}, u32[]{:S(2)}) %copy-start.1) | copy-done | bytes 152
  2.3 0.0 copy-start.2
  2.3 0.7 %copy-done.2 = s32[8,4]{0,1:T(4,128)S(1)} copy-done((s32[8,4]{0,1:T(4,128)S(1)}, s32[8,4]{0,1:T(4,128)}, u32[]{:S(2)}) %copy-start.2) | copy-done | bytes 152
  3.0 0.0 copy-start.3
  3.0 0.7 %copy-done.3 = s32[2,128]{1,0:T(2,128)S(1)} copy-done((s32[2,128]{1,0:T(2,128)S(1)}, s32[2,128]{1,0:T(2,128)}, u32[]{:S(2)}) %copy-start.3) | copy-done | bytes 1048
  3.6 8.6 %shard_map.55.half_ref = bf16[1024,2048]{1,0:T(8,128)(2,1)S(1)} custom-call(s32[4,8]{1,0:T(4,128)S(1)} %bitcast.2, s32[4,8]{1,0:T(4,128)S(1)} %bitcast.3, s32[2,128]{1,0:T(2,128)S(1)} %copy-done.3, bf16[512,2048]{1,0:T(8,128)(2,1)S(1)} %copy-done, bf16[8,8,4,128,128]{4,3,2,1,0:T(8,128)(2,1)} %fac_ref.1), custom_call_target="tpu_custom_call" | custom-call | flops 2147483648 | bytes 8388608 | tf_op jit(solution)/shard_map/pallas_call | solution.py:48
  12.3 50.4 %shard_map.56 = f32[1024,256]{1,0:T(8,128)S(1)} custom-call(bf16[1024,2048]{1,0:T(8,128)(2,1)S(1)} %shard_map.55.half_ref), custom_call_target="tpu_custom_call" | custom-call | flops 4294967296 | bytes 4194304 | tf_op jit(solution)/shard_map/pallas_call | solution.py:343
  62.7 1.0 %copy.7 = f32[1024,256]{1,0:T(8,128)} copy(f32[1024,256]{1,0:T(8,128)S(1)} %shard_map.56) | data formatting | bytes 2097152
Async XLA Ops:
  0.0 1.6 %copy-start = (bf16[512,2048]{1,0:T(8,128)(2,1)S(1)}, bf16[512,2048]{1,0:T(8,128)(2,1)}, u32[]{:S(2)}) copy-start(bf16[512,2048]{1,0:T(8,128)(2,1)} %coef_ref.1) | copy-start | bytes 6291460
  1.6 0.7 %copy-start.1 = (s32[8,4]{0,1:T(4,128)S(1)}, s32[8,4]{0,1:T(4,128)}, u32[]{:S(2)}) copy-start(s32[8,4]{0,1:T(4,128)} %param.6) | copy-start | bytes 388
  2.3 0.7 %copy-start.2 = (s32[8,4]{0,1:T(4,128)S(1)}, s32[8,4]{0,1:T(4,128)}, u32[]{:S(2)}) copy-start(s32[8,4]{0,1:T(4,128)} %param.7) | copy-start | bytes 388
  3.0 0.7 %copy-start.3 = (s32[2,128]{1,0:T(2,128)S(1)}, s32[2,128]{1,0:T(2,128)}, u32[]{:S(2)}) copy-start(s32[2,128]{1,0:T(2,128)} %rows_ref.1) | copy-start | bytes 3076

commit v3 on v2

--- a/solution.py
+++ b/solution.py
@@ -58,7 +58,7 @@
         ],
         out_specs=pl.BlockSpec((tile, depth), lambda t: (t, 0)),
         scratch_shapes=[pltpu.VMEM((batches * occ, coefficients.shape[1]), jnp.bfloat16)],
-        compiler_params=pltpu.CompilerParams(vmem_limit_bytes=40 * 2**20),
+        compiler_params=pltpu.CompilerParams(vmem_limit_bytes=60 * 2**20),
         cost_estimate=pl.CostEstimate(flops=2 * factors.size * batches * occ, bytes_accessed=factors.size * 2, transcendentals=0),
     )(tile_cols.T, tile_live.T, batch_rows, coefficients, factors)
 
@@ -87,11 +87,18 @@
     own_copy = pltpu.make_async_copy(half_ref, h.at[mine], own_sem)
     own_copy.start()
     pl.semaphore_wait(barrier, 15)
-    swap = pltpu.make_async_remote_copy(
-        src_ref=half_ref, dst_ref=h.at[mine], send_sem=h_send, recv_sem=h_recv,
-        device_id=(g, aux, 1 - b), device_id_type=MESH,
-    )
-    swap.start()
+
+    def swap(q):
+        return pltpu.make_async_remote_copy(
+            src_ref=half_ref.at[pl.ds(pl.multiple_of(q * 512, 512), 512)],
+            dst_ref=h.at[pl.ds(pl.multiple_of(b * rows + q * 512, 512), 512)],
+            send_sem=h_send.at[q], recv_sem=h_recv.at[q],
+            device_id=(g, aux, 1 - b), device_id_type=MESH,
+        )
+
+    ahead = jnp.where(b == 1, jnp.where(z == 3, 0, 1), jnp.where(z == 0, 1, 0))
+    swap(ahead).start()
+    swap(1 - ahead).start()
 
     diagonal = lax.broadcasted_iota(jnp.int32, (128, 128), 0) == lax.broadcasted_iota(jnp.int32, (128, 128), 1)
     row_ids = lax.broadcasted_iota(jnp.int32, (128, 128), 0)
@@ -147,11 +154,12 @@
         return lax.dot_general(left, right, LAST, preferred_element_type=jnp.float32)
 
     def compute_step(s, carry):
-        @pl.when(s == 1)
-        def _():
-            swap.wait()
-
         zd = dest(s)
+
+        @pl.when(jnp.logical_not(extra(zd)))
+        def _():
+            swap(lax.rem(zd, 2)).wait_recv()
+
         theirs, ours = zd * 2 + 1 - y, zd * 2 + y
         starts = [b * 4 + j for j in range(4)]
 
@@ -209,7 +217,6 @@
 
         return carry
 
-    lax.fori_loop(0, 4, compute_step, 0)
 
     def add(s, c, ref):
         at, size = CHUNKS[c]
@@ -244,7 +251,15 @@
         each_chunk(zd, chunk)
         return carry
 
-    lax.fori_loop(0, 3, chain_step, 0)
+    end = jnp.logical_or(z == 0, z == 3)
+    lax.fori_loop(0, 2, compute_step, 0)
+
+    @pl.when(end)
+    def _():
+        chain_step(0, 0)
+
+    lax.fori_loop(2, 4, compute_step, 0)
+    lax.fori_loop(jnp.where(end, 1, 0), 3, chain_step, 0)
 
     def f_copy(j, to, to_core, slot_at):
         return pltpu.make_async_remote_copy(
@@ -328,6 +343,8 @@
         return carry
 
     lax.fori_loop(0, 4, drain, 0)
+    swap(0).wait_send()
+    swap(1).wait_send()
     for j in range(4):
         r = b * 4 + j
 
@@ -355,10 +372,10 @@
             pltpu.VMEM((2, 4, 640, 256), bf16),
             pltpu.VMEM((4, 128, 256), bf16),
             pltpu.VMEM((4, 128, 256), bf16),
-            dma, dma, dma, dma((4, 3)), dma((4, 3)), dma((4, 3)), dma((2, 4, 3)), dma((4,)), dma((4,)),
+            dma, dma((2,)), dma((2,)), dma((4, 3)), dma((4, 3)), dma((4, 3)), dma((2, 4, 3)), dma((4,)), dma((4,)),
         ],
         compiler_params=pltpu.CompilerParams(
-            collective_id=0, has_side_effects=True, vmem_limit_bytes=48 * 2**20
+            collective_id=0, has_side_effects=True, vmem_limit_bytes=60 * 2**20
         ),
         cost_estimate=pl.CostEstimate(flops=2 * rows * rows * depth, bytes_accessed=half.size * 2, transcendentals=0),
     )(half)

time: 64.8 us -> 61.1 us (0.943); the launches traced: 63.6 us -> 60.8 us
  local copies, waits for them, and re-layouts: 4.6 us -> 2.26 us
    pallas_call x1, Pallas kernels: 50.4 us -> 47.8 us  [exchange(): pl.pallas_call(functools.partial(exchange_kernel, norm), out_shape=jax.Sh...]
    unnamed x9 -> x1, local copies, waits for them, and re-layouts: 4.6 us -> 2.26 us
    pallas_call x1, Pallas kernels: 8.65 us -> 10.7 us  [half_transformed(): pl.pallas_call(half_kernel, grid=(tiles,), out_shape=jax.ShapeDtypeStruct...]
where the time goes in v3:
time: 61.1 us; the launch traced here: 60.8 us
  Pallas kernels  58.5 us (96%)
  local copies, waits for them, and re-layouts  2.26 us (4%)
    pallas_call x1, Pallas kernels, exchange(): pl.pallas_call(functools.partial(exchange_kernel, norm), out_shape=jax.Sh...  47.8 us
    pallas_call x1, Pallas kernels, half_transformed(): pl.pallas_call(half_kernel, grid=(tiles,), out_shape=jax.ShapeDtypeStruct...  10.7 us
    unnamed x1, local copies, waits for them, and re-layouts  2.26 us

profile of v3, /device:TPU:9, one launch (start us, length us, event | category | flops | bytes accessed | tf_op | source)
XLA Modules:
  0.0 60.8 jit_solution(12299896105576978739)
XLA Ops:
  0.0 10.7 %shard_map.55.half_ref = bf16[1024,2048]{1,0:T(8,128)(2,1)} custom-call(s32[4,8]{1,0:T(4,128)} %bitcast.2, s32[4,8]{1,0:T(4,128)} %bitcast.3, s32[2,128]{1,0:T(2,128)} %rows_ref.1, bf16[512,2048]{1,0:T(8,128)(2,1)} %coef_ref.1, bf16[8,8,4,128,128]{4,3,2,1,0:T(8,128)(2,1)} %fac_ref.1), custom_call_target="tpu_custom_call" | custom-call | flops 2147483648 | bytes 8388608 | tf_op jit(solution)/shard_map/pallas_call | solution.py:48
  10.8 47.8 %shard_map.56 = f32[1024,256]{1,0:T(8,128)} custom-call(bf16[1024,2048]{1,0:T(8,128)(2,1)} %shard_map.55.half_ref), custom_call_target="tpu_custom_call" | custom-call | flops 4294967296 | bytes 4194304 | tf_op jit(solution)/shard_map/pallas_call | solution.py:360
  58.5 2.3 %copy.7 = f32[1024,256]{1,0:T(8,128)} copy(f32[1024,256]{1,0:T(8,128)} %shard_map.56) | data formatting | bytes 2097152

commit v4 on v3

--- a/solution.py
+++ b/solution.py
@@ -375,7 +375,7 @@
             dma, dma((2,)), dma((2,)), dma((4, 3)), dma((4, 3)), dma((4, 3)), dma((2, 4, 3)), dma((4,)), dma((4,)),
         ],
         compiler_params=pltpu.CompilerParams(
-            collective_id=0, has_side_effects=True, vmem_limit_bytes=60 * 2**20
+            collective_id=0, has_side_effects=True, vmem_limit_bytes=52 * 2**20
         ),
         cost_estimate=pl.CostEstimate(flops=2 * rows * rows * depth, bytes_accessed=half.size * 2, transcendentals=0),
     )(half)

time: 61.1 us -> 58.8 us (0.962)
  local copies, waits for them, and re-layouts: 2.26 us -> 0.97 us
  Pallas kernels: 58.5 us -> 57.5 us
    unnamed x1, local copies, waits for them, and re-layouts: 2.26 us -> 0.97 us
    pallas_call x1, Pallas kernels: 47.8 us -> 46.8 us  [exchange(): pl.pallas_call(functools.partial(exchange_kernel, norm), out_shape=jax.Sh...]
where the time goes in v4:
time: 58.8 us; the launch traced here: 58.5 us
  Pallas kernels  57.5 us (98%)
  local copies, waits for them, and re-layouts  0.97 us (2%)
    pallas_call x1, Pallas kernels, exchange(): pl.pallas_call(functools.partial(exchange_kernel, norm), out_shape=jax.Sh...  46.8 us
    pallas_call x1, Pallas kernels, half_transformed(): pl.pallas_call(half_kernel, grid=(tiles,), out_shape=jax.ShapeDtypeStruct...  10.8 us

profile of v4, /device:TPU:9, one launch (start us, length us, event | category | flops | bytes accessed | tf_op | source)
XLA Modules:
  0.0 58.5 jit_solution(1329551565833612196)
XLA Ops:
  0.0 10.8 %shard_map.55.half_ref = bf16[1024,2048]{1,0:T(8,128)(2,1)} custom-call(s32[4,8]{1,0:T(4,128)} %bitcast.2, s32[4,8]{1,0:T(4,128)} %bitcast.3, s32[2,128]{1,0:T(2,128)} %rows_ref.1, bf16[512,2048]{1,0:T(8,128)(2,1)} %coef_ref.1, bf16[8,8,4,128,128]{4,3,2,1,0:T(8,128)(2,1)} %fac_ref.1), custom_call_target="tpu_custom_call" | custom-call | flops 2147483648 | bytes 8388608 | tf_op jit(solution)/shard_map/pallas_call | solution.py:48
  10.8 46.8 %shard_map.56 = f32[1024,256]{1,0:T(8,128)S(1)} custom-call(bf16[1024,2048]{1,0:T(8,128)(2,1)} %shard_map.55.half_ref), custom_call_target="tpu_custom_call" | custom-call | flops 4294967296 | bytes 4194304 | tf_op jit(solution)/shard_map/pallas_call | solution.py:360
  57.5 1.0 %copy.7 = f32[1024,256]{1,0:T(8,128)} copy(f32[1024,256]{1,0:T(8,128)S(1)} %shard_map.56) | data formatting | bytes 2097152
